TPU v7x, 32 devices: a whole 2x2x4 slice. The times are simulated.
32 devices in a mesh: leaf: 32 (over z, y, x, core).
Axes of the slice: x: 2, y: 2, z: 4, core: 2. Of those that a mesh axis runs over, the one named last changes fastest.
Arguments:
- points: bfloat16 [128, 262144], P(None, 'leaf')
- probes: bfloat16 [16, 262144], P(None, 'leaf'), may hold values from -6 to 6
- near_list: int32 [512, 4], P('leaf'), may hold values from 0 to 511, as said below
- near_count: int32 [512], P('leaf'), may hold values from 1 to 4, as said below
- leaf_skel: int32 [512, 128], P('leaf'), may hold values from 0 to 511, as said below
- local_skel: int32 [480, 128], P('leaf'), may hold values from 0 to 255, as said below
- upper_skel: int32 [31, 128], replicated, may hold values from 0 to 255, as said below
Outputs:
- response: float32 [16, 262144], P(None, 'leaf')
Inputs may be any that keep to these rules, and one draw needn't show every extreme that they name: `near_list`: entry 0 of leaf t's list is t itself; every entry is a leaf of the same block of 16 consecutive leaves as t, or of the block just before or just after it. `near_count`: some leaf uses all 4 slots. `leaf_skel`: each row holds 128 distinct values. `local_skel`: each row holds 128 distinct values. `upper_skel`: each row holds 128 distinct values.
All inputs are finite; a program needn't handle non-finite values.
Results may differ from a plain program's by a relative error of at most 0.0015.
Values may be sent and summed in bfloat16 or wider, within the bound.
A program may use at most 128 MiB of HBM per device.

v0:
```python
import functools
import math

import jax
import jax.numpy as jnp
from jax import lax
from jax.experimental import pallas as pl
from jax.experimental.pallas import tpu as pltpu
from jax.sharding import PartitionSpec as P

F32 = jnp.float32
BF16 = jnp.bfloat16
DEEP = 256
PIECE = 16
PAIRS = 2
VMEM_LIMIT = 56 * 1024 * 1024


def mm(left, right):
    return jnp.dot(left, right, preferred_element_type=F32)


def mm_nt(left, right):
    return lax.dot_general(left, right, (((1,), (1,)), ((), ())), preferred_element_type=F32)


def split(value):
    high = value.astype(BF16)
    low = (value - high.astype(F32)).astype(BF16)
    return high, low


def affinity(scaled, emb_width):
    return jnp.exp2(scaled * (4.0 / emb_width * math.log2(math.e)))


def half_norms(pts):
    wide = pts.astype(F32)
    value = jnp.sum(wide * wide, axis=0, keepdims=True) * -0.5
    first = value.astype(BF16).astype(F32)
    rest = value - first
    second = rest.astype(BF16).astype(F32)
    third = (rest - second).astype(BF16).astype(F32)
    return first, second, third


def norm_rows(pieces, start):
    width = pieces[0].shape[1]
    row = lax.broadcasted_iota(jnp.int32, (PIECE, width), 0)
    rows = jnp.where(row < 6, 1.0, 0.0)
    for k, piece in enumerate(pieces):
        rows = jnp.where(row == start + k, piece, rows)
    return rows.astype(BF16)


def deep(*blocks):
    rows = sum(block.shape[0] for block in blocks)
    filler = jnp.zeros((DEEP - rows, blocks[0].shape[1]), BF16)
    return jnp.concatenate([*blocks, filler], axis=0)


def one_hot(pool, chosen):
    column = lax.broadcasted_iota(jnp.int32, (pool, chosen.shape[1]), 0)
    return jnp.where(column == chosen, 1.0, 0.0).astype(BF16)


def in_groups(total, size, step):
    size = min(size, total)
    if size == total:
        step(list(range(total)))
        return

    def body(i, carry):
        step([i * size + k for k in range(size)])
        return carry

    lax.fori_loop(0, total // size, body, 0)


def tree_node(first, second, first_q, second_q, chosen, emb_width, coupled):
    skel = first.shape[1]
    right_end = emb_width + PIECE
    joined = jnp.concatenate([first, second], axis=1)
    parent = mm(joined, one_hot(2 * skel, chosen)).astype(BF16)
    left = deep(joined[:emb_width], joined[right_end:]).T
    if coupled:
        right = deep(jnp.concatenate([parent[:right_end], second[:right_end]], axis=1))
    else:
        right = deep(parent[:right_end])
    raw = mm(left, right)
    up_high, up_low = split(affinity(raw[:, :skel], emb_width))
    joined_q = jnp.concatenate([first_q, second_q], axis=1)
    parent_q = (mm(joined_q, up_high) + mm(joined_q, up_low)).astype(BF16)
    if not coupled:
        return parent, parent_q
    cross_high, cross_low = split(affinity(raw[:skel, skel:], emb_width))
    couple_first = mm_nt(second_q, cross_high) + mm_nt(second_q, cross_low)
    couple_second = mm(first_q, cross_high) + mm(first_q, cross_low)
    return parent, parent_q, up_high, up_low, couple_first, couple_second


def spread_down(field, up_high, up_low):
    rows = field.shape[0]
    high, low = split(field)
    both = mm_nt(jnp.concatenate([high, low], axis=0), up_high)
    return both[:rows] + both[rows:] + mm_nt(high, up_low)


def up_body(pts, prb, leaf_skel, local_skel, left_out, right_out, lk_high, lk_low, up_high, up_low, couple, root, nodes, node_q):
    emb_width = pts.shape[0]
    leaf_dev, skel = leaf_skel.shape
    leaf_len = pts.shape[1] // leaf_dev

    def leaf_step(ids):
        done = []
        for i in ids:
            span = pl.ds(pl.multiple_of(i * leaf_len, leaf_len), leaf_len)
            tile = pts[:, span]
            pieces = half_norms(tile)
            right_rows = norm_rows(pieces, 3)
            left_rows = norm_rows(pieces, 0)
            left = deep(tile, left_rows).T
            stacked = jnp.concatenate([tile, right_rows, left_rows], axis=0)
            node = mm(stacked, one_hot(leaf_len, leaf_skel[pl.ds(i, 1), :])).astype(BF16)
            raw = mm(left, deep(node[: emb_width + PIECE]))
            high, low = split(affinity(raw, emb_width))
            tile_prb = prb[:, span]
            charge = (mm(tile_prb, high) + mm(tile_prb, low)).astype(BF16)
            done.append((span, right_rows, left, node, high, low, charge))
        for i, (span, right_rows, left, node, high, low, charge) in zip(ids, done):
            left_out[span, :] = left
            right_out[:, span] = right_rows
            lk_high[span, :] = high
            lk_low[span, :] = low
            nodes[i] = node
            node_q[i] = charge

    in_groups(leaf_dev, 4, leaf_step)
    count = leaf_dev // 2
    row_base = 0
    while count:

        def level_step(ids, row_base=row_base):
            done = []
            for k in ids:
                row = row_base + k
                done.append(
                    tree_node(
                        nodes[2 * row], nodes[2 * row + 1], node_q[2 * row], node_q[2 * row + 1],
                        local_skel[pl.ds(row, 1), :], emb_width, True,
                    )
                )
            for k, (parent, parent_q, high, low, one, two) in zip(ids, done):
                row = row_base + k
                nodes[leaf_dev + row] = parent
                node_q[leaf_dev + row] = parent_q
                up_high[row] = high
                up_low[row] = low
                couple[2 * row] = one
                couple[2 * row + 1] = two

        in_groups(count, 4, level_step)
        row_base += count
        count //= 2
    top = 2 * leaf_dev - 2
    rows = nodes.shape[1]
    root[:rows, :] = nodes[top]
    root[rows:, :] = node_q[top]


def list_pairs(near_list, near_count, base, leaf_dev, targets, sources):
    def of_leaf(leaf, found):
        def of_slot(slot, found):
            source = near_list[leaf, slot] - base
            targets[found] = leaf
            sources[found] = jnp.clip(source, 0, leaf_dev - 1)
            inside = jnp.logical_and(source >= 0, source < leaf_dev)
            return found + jnp.where(inside, 1, 0)

        return lax.fori_loop(0, near_count[leaf], of_slot, found)

    found = lax.fori_loop(0, leaf_dev, of_leaf, 0)
    for k in range(PAIRS - 1):
        targets[found + k] = leaf_dev
        sources[found + k] = 0
    return (found + PAIRS - 1) // PAIRS


def add_pairs(steps, targets, sources, left, pts, rows, prb, total):
    emb_width = pts.shape[0]
    leaf_dev = total.shape[0] - 1
    leaf_len = total.shape[2]
    chunk = min(256, leaf_len)

    def step(i, carry):
        done = []
        for k in range(PAIRS):
            target = targets[i * PAIRS + k]
            start = pl.multiple_of(sources[i * PAIRS + k] * leaf_len, leaf_len)
            span = pl.ds(start, leaf_len)
            right = deep(pts[:, span], rows[:, span])
            source_prb = prb[:, span]
            left_at = jnp.minimum(target, leaf_dev - 1) * leaf_len
            for at in range(0, leaf_len, chunk):
                part = left[pl.ds(pl.multiple_of(left_at + at, chunk), chunk), :]
                block = affinity(mm(part, right), emb_width).astype(BF16)
                done.append((target, at, mm_nt(source_prb, block)))
        for target, at, term in done:
            total[target, :, at : at + chunk] += term
        return carry

    lax.fori_loop(0, steps, step, 0)


def near_own_body(me, near_list, near_count, left, pts, rows, prb, total, targets, sources):
    leaf_dev = near_list.shape[0]
    total[...] = jnp.zeros_like(total)
    steps = list_pairs(near_list, near_count, me[0] * leaf_dev, leaf_dev, targets, sources)
    add_pairs(steps, targets, sources, left, pts, rows, prb, total)


def near_halo_body(me, near_list, near_count, left, pts_a, prb_a, pts_b, prb_b, so_far, far, out, total, rows_a, rows_b, targets, sources):
    leaf_dev = near_list.shape[0]
    leaf_len = total.shape[2]
    total[...] = so_far[...]
    for pts, rows in ((pts_a, rows_a), (pts_b, rows_b)):

        def norms(ids, pts=pts, rows=rows):
            for i in ids:
                span = pl.ds(pl.multiple_of(i * leaf_len, leaf_len), leaf_len)
                rows[:, span] = norm_rows(half_norms(pts[:, span]), 3)

        in_groups(leaf_dev, 2, norms)
    for shift, pts, rows, prb in ((-1, pts_a, rows_a, prb_a), (1, pts_b, rows_b, prb_b)):
        steps = list_pairs(near_list, near_count, (me[0] + shift) * leaf_dev, leaf_dev, targets, sources)
        add_pairs(steps, targets, sources, left, pts, rows, prb, total)
    for leaf in range(leaf_dev):
        span = slice(leaf * leaf_len, (leaf + 1) * leaf_len)
        out[:, span] = total[leaf] + far[:, span]


def down_body(emb_width, me, roots, upper_skel, lk_high, lk_low, up_high, up_low, couple, far, nodes, path_high, path_low, path_couple, fields):
    dev_num = roots.shape[0]
    skel = upper_skel.shape[1]
    pts_rows = emb_width + 2 * PIECE
    leaf_dev = couple.shape[0] // 2 + 1
    leaf_len = lk_high.shape[0] // leaf_dev
    mine = me[0]
    levels = dev_num.bit_length() - 1
    for level in range(levels):
        row_base = dev_num - (dev_num >> level)
        children = roots if level == 0 else nodes
        child_base = 0 if level == 0 else dev_num - (dev_num >> (level - 1))

        def operands(k, level=level, row_base=row_base, children=children, child_base=child_base):
            one = children[child_base + 2 * k]
            two = children[child_base + 2 * k + 1]
            chosen = upper_skel[pl.ds(row_base + k, 1), :]
            return one[:pts_rows], two[:pts_rows], one[pts_rows:], two[pts_rows:], chosen

        spot = jnp.right_shift(mine, level + 1)
        bit = jnp.bitwise_and(jnp.right_shift(mine, level), 1)
        _, _, high, low, couple_one, couple_two = tree_node(*operands(spot), emb_width, True)
        path_high[level] = high
        path_low[level] = low
        path_couple[level] = jnp.where(bit == 0, couple_one, couple_two)

        if level < levels - 1:

            def level_step(ids, row_base=row_base, operands=operands):
                done = [tree_node(*operands(k), emb_width, False) for k in ids]
                for k, (parent, parent_q) in zip(ids, done):
                    nodes[row_base + k, :pts_rows, :] = parent
                    nodes[row_base + k, pts_rows:, :] = parent_q

            in_groups(dev_num >> (level + 1), 4, level_step)
    field = jnp.zeros(path_couple.shape[1:], F32)
    for level in reversed(range(levels)):
        bit = jnp.bitwise_and(jnp.right_shift(mine, level), 1)
        spread = spread_down(field, path_high[level], path_low[level])
        field = jnp.where(bit == 0, spread[:, :skel], spread[:, skel:]) + path_couple[level]
    top = 2 * leaf_dev - 2
    fields[top] = field
    count = 1
    row_base = leaf_dev - 2
    while count < leaf_dev:

        def level_step(ids, row_base=row_base):
            done = []
            for k in ids:
                row = row_base + k
                spread = spread_down(fields[leaf_dev + row], up_high[row], up_low[row])
                done.append((spread[:, :skel] + couple[2 * row], spread[:, skel:] + couple[2 * row + 1]))
            for k, (one, two) in zip(ids, done):
                fields[2 * (row_base + k)] = one
                fields[2 * (row_base + k) + 1] = two

        in_groups(count, 4, level_step)
        count *= 2
        row_base -= count

    def leaf_step(ids):
        for i in ids:
            span = pl.ds(pl.multiple_of(i * leaf_len, leaf_len), leaf_len)
            far[:, span] = spread_down(fields[i], lk_high[span, :], lk_low[span, :])

    in_groups(leaf_dev, 4, leaf_step)


def shape(dims, dtype):
    return jax.ShapeDtypeStruct(tuple(dims), dtype)


def call(body, name, operands, outs, scratch, scalars, flops, exps):
    vmem = pl.BlockSpec(memory_space=pltpu.VMEM)
    smem = pl.BlockSpec(memory_space=pltpu.SMEM)
    moved = sum(x.size * x.dtype.itemsize for x in [*operands, *outs])
    return pl.pallas_call(
        body,
        out_shape=outs,
        in_specs=[smem] * scalars + [vmem] * (len(operands) - scalars),
        out_specs=[vmem] * len(outs),
        scratch_shapes=scratch,
        compiler_params=pltpu.CompilerParams(vmem_limit_bytes=VMEM_LIMIT),
        cost_estimate=pl.CostEstimate(flops=flops, bytes_accessed=moved, transcendentals=exps),
        name=name,
    )(*operands)


def per_device(points, probes, near_list, near_count, leaf_skel, local_skel, upper_skel):
    emb_width, shard_len = points.shape
    leaf_dev, slots = near_list.shape
    leaf_len = shard_len // leaf_dev
    skel = leaf_skel.shape[1]
    probe_num = probes.shape[0]
    dev_num = lax.axis_size("leaf")
    levels = dev_num.bit_length() - 1
    me = lax.axis_index("leaf").astype(jnp.int32).reshape(1)
    rise = [(i, i + 1) for i in range(dev_num - 1)]
    fall = [(i + 1, i) for i in range(dev_num - 1)]
    pts_a = lax.ppermute(points, "leaf", rise)
    prb_a = lax.ppermute(probes, "leaf", rise)
    pts_b = lax.ppermute(points, "leaf", fall)
    prb_b = lax.ppermute(probes, "leaf", fall)

    low_nodes = leaf_dev - 1
    all_nodes = 2 * leaf_dev - 1
    pts_rows = emb_width + 2 * PIECE
    left, rows, lk_high, lk_low, up_high, up_low, couple, root = call(
        up_body,
        "leaf_up",
        [points, probes, leaf_skel, local_skel],
        [
            shape((shard_len, DEEP), BF16),
            shape((PIECE, shard_len), BF16),
            shape((shard_len, skel), BF16),
            shape((shard_len, skel), BF16),
            shape((low_nodes, 2 * skel, skel), BF16),
            shape((low_nodes, 2 * skel, skel), BF16),
            shape((2 * low_nodes, probe_num, skel), F32),
            shape((pts_rows + probe_num, skel), BF16),
        ],
        [pltpu.VMEM((all_nodes, pts_rows, skel), BF16), pltpu.VMEM((all_nodes, probe_num, skel), BF16)],
        0,
        8 * shard_len * skel * DEEP,
        shard_len * skel * 2,
    )
    roots = lax.all_gather(root, "leaf")

    pair_len = slots * leaf_dev + PAIRS
    lists = [pltpu.SMEM((pair_len,), jnp.int32), pltpu.SMEM((pair_len,), jnp.int32)]
    pair_cost = 4 * leaf_len * leaf_len * DEEP
    (near_own,) = call(
        near_own_body,
        "near_own",
        [me, near_list, near_count, left, points, rows, probes],
        [shape((leaf_dev + 1, probe_num, leaf_len), F32)],
        lists,
        3,
        pair_cost * leaf_dev * 2,
        leaf_len * leaf_len * leaf_dev * 2,
    )
    (far,) = call(
        functools.partial(down_body, emb_width),
        "tree_down",
        [me, roots, upper_skel, lk_high, lk_low, up_high, up_low, couple],
        [shape((probe_num, shard_len), F32)],
        [
            pltpu.VMEM((dev_num, pts_rows + probe_num, skel), BF16),
            pltpu.VMEM((levels, 2 * skel, skel), BF16),
            pltpu.VMEM((levels, 2 * skel, skel), BF16),
            pltpu.VMEM((levels, probe_num, skel), F32),
            pltpu.VMEM((all_nodes, probe_num, skel), F32),
        ],
        1,
        8 * shard_len * skel * DEEP,
        shard_len * skel,
    )
    (response,) = call(
        near_halo_body,
        "near_halo",
        [me, near_list, near_count, left, pts_a, prb_a, pts_b, prb_b, near_own, far],
        [shape((probe_num, shard_len), F32)],
        [
            pltpu.VMEM((leaf_dev + 1, probe_num, leaf_len), F32),
            pltpu.VMEM((PIECE, shard_len), BF16),
            pltpu.VMEM((PIECE, shard_len), BF16),
            *lists,
        ],
        3,
        pair_cost * leaf_dev * 2,
        leaf_len * leaf_len * leaf_dev * 2,
    )
    return response


def solution(mesh):
    in_specs = (
        P(None, "leaf"),
        P(None, "leaf"),
        P("leaf", None),
        P("leaf"),
        P("leaf", None),
        P("leaf", None),
        P(),
    )
    return jax.shard_map(
        per_device, mesh=mesh, in_specs=in_specs, out_specs=P(None, "leaf"), check_vma=False
    )
```

profile of v0, /device:TPU:16, one launch (start us, length us, event | category | flops | bytes accessed | tf_op | source)
XLA Modules:
  0.0 130.3 jit_solution(1537016264365872418)
XLA Ops:
  6.5 0.0 copy-start.1
  6.5 0.0 copy-start.2
  6.5 0.0 copy-start
  6.5 0.0 all-gather.3.cloned.1.call-start
  6.5 18.1 %leaf_up.1 = (bf16[8192,256]{1,0:T(8,128)(2,1)}, bf16[16,8192]{1,0:T(8,128)(2,1)}, bf16[8192,128]{1,0:T(8,128)(2,1)}, bf16[8192,128]{1,0:T(8,128)(2,1)}, bf16[15...) custom-call(bf16[128,8192]{1,0:T(8,128)(2,1)} %pts.3, ...), custom_call_target="tpu_custom_call" | custom-call | flops 2147483648 | bytes 13282816 | tf_op jit(solution)/shard_map/leaf_up/pallas_call | solution.py:318
  24.6 0.0 all-gather.3.cloned.1.call-update
  24.6 0.0 copy-done.1
  24.6 1.9 %collective-permute-start = (bf16[128,8192]{1,0:T(8,128)(2,1)S(1)}, bf16[128,8192]{1,0:T(8,128)(2,1)}, u32[]{:S(2)}, u32[]{:S(2)}) collective-permute-start(bf16[128,8192]{1,0:T(8,128)(2,1)S(1)} %copy-done.1), channel_id=1, source_target_pairs={{0,1},{1,2},{2,3},{3,4},{4,5},{5,6},{6,7},{7,8},{8,9},{9,10},{10,1... | collective-permute-start | bytes 6291464 | tf_op jit(solution)/shard_map/ppermute | solution.py:341
  26.6 5.4 %collective-permute-start.2 = (bf16[128,8192]{1,0:T(8,128)(2,1)S(1)}, bf16[128,8192]{1,0:T(8,128)(2,1)}, u32[]{:S(2)}, u32[]{:S(2)}) collective-permute-start(bf16[128,8192]{1,0:T(8,128)(2,1)S(1)} %copy-done.1), channel_id=1, source_target_pairs={{1,0},{2,1},{3,2},{4,3},{5,4},{6,5},{7,6},{8,7},{9,8},{10,9},{11,1... | collective-permute-start | bytes 6291464 | tf_op jit(solution)/shard_map/ppermute | solution.py:343
  32.0 0.0 copy-done.2
  32.0 1.9 %collective-permute-start.1 = (bf16[16,8192]{1,0:T(8,128)(2,1)S(1)}, bf16[16,8192]{1,0:T(8,128)(2,1)S(1)}, u32[]{:S(2)}, u32[]{:S(2)}) collective-permute-start(bf16[16,8192]{1,0:T(8,128)(2,1)S(1)} %copy-done.2), channel_id=1, source_target_pairs={{0,1},{1,2},{2,3},{3,4},{4,5},{5,6},{6,7},{7,8},{8,9},{9,10},{10,1... | collective-permute-start | bytes 786440 | tf_op jit(solution)/shard_map/ppermute | solution.py:342
  33.9 5.4 %collective-permute-start.3 = (bf16[16,8192]{1,0:T(8,128)(2,1)S(1)}, bf16[16,8192]{1,0:T(8,128)(2,1)S(1)}, u32[]{:S(2)}, u32[]{:S(2)}) collective-permute-start(bf16[16,8192]{1,0:T(8,128)(2,1)S(1)} %copy-done.2), channel_id=1, source_target_pairs={{1,0},{2,1},{3,2},{4,3},{5,4},{6,5},{7,6},{8,7},{9,8},{10,9},{11,1... | collective-permute-start | bytes 786440 | tf_op jit(solution)/shard_map/ppermute | solution.py:344
  39.4 0.0 copy-done
  39.4 0.7 copy.9.near_list
  40.1 10.4 %near_own.1.so_far = f32[17,16,512]{2,1,0:T(8,128)} custom-call(s32[1]{0:T(128)} %bitcast.me, s32[16,4]{1,0:T(8,128)} %copy.9.near_list, s32[16]{0:T(128)} %near_count.3, bf16[8192,256]{1,0:T(8,128)(2,1)} %get-tuple-element.13.left, bf16[128,8192]{1,0:T(8,128)(2,1)} %pts.3, bf16[16,8192]{1,0:T(8,128)(2,1)} %get-tuple-element.14.rows, bf16[16,8192]{1,0:T(8,128)(2,1)} %prb.3), custom_call_target="tpu_custom_call" | custom-call | flops 8589934592 | bytes 7373124 | tf_op jit(solution)/shard_map/near_own/pallas_call | solution.py:318
  50.5 37.5 %all-gather.3.cloned.1.call-done = bf16[5632,128]{1,0:T(8,128)(2,1)} async-done(((bf16[176,128]{1,0:T(8,128)(2,1)}), bf16[5632,128]{1,0:T(8,128)(2,1)}) %all-gather.3.cloned.1.call-update) | async-done | bytes 1441808 | tf_op jit(solution)/shard_map/all_gather | solution.py:368
  88.0 18.9 %tree_down.1.far = f32[16,8192]{1,0:T(8,128)} custom-call(s32[1]{0:T(128)} %bitcast.me, bf16[32,176,128]{2,1,0:T(8,128)(2,1)} %bitcast.2, s32[31,128]{1,0:T(8,128)} %upper_skel.1, bf16[8192,128]{1,0:T(8,128)(2,1)} %get-tuple-element.16.lk_high, bf16[8192,128]{1,0:T(8,128)(2,1)} %get-tuple-element.17.lk_low, bf16[15,256,128]{2,1,0:T(8,128)(2,1)} %get-tuple-element.18.up_high, ...), custom_call_target="tpu_custom_call" | custom-call | flops 2147483648 | bytes 8388100 | tf_op jit(solution)/shard_map/tree_down/pallas_call | solution.py:318
  106.9 0.0 collective-permute-done.1.prb_a
  107.0 0.0 copy-start.3
  107.0 0.0 collective-permute-done.3.prb_b
  107.0 0.0 copy-start.4
  107.0 0.0 collective-permute-done.pts_a
  107.0 0.0 collective-permute-done.2.pts_b
  107.0 0.7 copy-done.3
  107.7 0.1 copy-done.4
  107.8 15.7 %near_halo.1 = f32[16,8192]{1,0:T(8,128)} custom-call(s32[1]{0:T(128)} %bitcast.me, s32[16,4]{1,0:T(8,128)} %copy.9.near_list, s32[16]{0:T(128)} %near_count.3, bf16[8192,256]{1,0:T(8,128)(2,1)} %get-tuple-element.13.left, bf16[128,8192]{1,0:T(8,128)(2,1)} %collective-permute-done.pts_a, bf16[16,8192]{1,0:T(8,128)(2,1)} %copy-done.3, ...), custom_call_target="tpu_custom_call" | custom-call | flops 8589934592 | bytes 10518852 | tf_op jit(solution)/shard_map/near_halo/pallas_call | solution.py:318
Async XLA Ops:
  6.5 18.1 %copy-start.1 = (bf16[128,8192]{1,0:T(8,128)(2,1)S(1)}, bf16[128,8192]{1,0:T(8,128)(2,1)}, u32[]{:S(2)}) copy-start(bf16[128,8192]{1,0:T(8,128)(2,1)} %pts.3) | copy-start | bytes 6291460
  6.5 25.5 %copy-start.2 = (bf16[16,8192]{1,0:T(8,128)(2,1)S(1)}, bf16[16,8192]{1,0:T(8,128)(2,1)}, u32[]{:S(2)}) copy-start(bf16[16,8192]{1,0:T(8,128)(2,1)} %prb.3) | copy-start | bytes 786436
  6.5 32.9 %copy-start = (s32[16,4]{0,1:T(4,128)S(1)}, s32[16,4]{0,1:T(4,128)}, u32[]{:S(2)}) copy-start(s32[16,4]{0,1:T(4,128)} %param.9) | copy-start | bytes 772
  6.5 81.5 %all-gather.3.cloned.1.call-start = ((), (), s32[]{:S(2)}) async-start(), calls=%async_computation | async-start | bytes 1486848 | tf_op jit(solution)/shard_map/all_gather | solution.py:368
  24.6 82.3 %collective-permute-start = (bf16[128,8192]{1,0:T(8,128)(2,1)S(1)}, bf16[128,8192]{1,0:T(8,128)(2,1)}, u32[]{:S(2)}, u32[]{:S(2)}) collective-permute-start(bf16[128,8192]{1,0:T(8,128)(2,1)S(1)} %copy-done.1), channel_id=1, source_target_pairs={{0,1},{1,2},{2,3},{3,4},{4,5},{5,6},{6,7},{7,8},{8,9},{9,10},{10,1... | collective-permute-start | bytes 6291464 | tf_op jit(solution)/shard_map/ppermute | solution.py:341
  26.6 80.4 %collective-permute-start.2 = (bf16[128,8192]{1,0:T(8,128)(2,1)S(1)}, bf16[128,8192]{1,0:T(8,128)(2,1)}, u32[]{:S(2)}, u32[]{:S(2)}) collective-permute-start(bf16[128,8192]{1,0:T(8,128)(2,1)S(1)} %copy-done.1), channel_id=1, source_target_pairs={{1,0},{2,1},{3,2},{4,3},{5,4},{6,5},{7,6},{8,7},{9,8},{10,9},{11,1... | collective-permute-start | bytes 6291464 | tf_op jit(solution)/shard_map/ppermute | solution.py:343
  32.0 74.9 %collective-permute-start.1 = (bf16[16,8192]{1,0:T(8,128)(2,1)S(1)}, bf16[16,8192]{1,0:T(8,128)(2,1)S(1)}, u32[]{:S(2)}, u32[]{:S(2)}) collective-permute-start(bf16[16,8192]{1,0:T(8,128)(2,1)S(1)} %copy-done.2), channel_id=1, source_target_pairs={{0,1},{1,2},{2,3},{3,4},{4,5},{5,6},{6,7},{7,8},{8,9},{9,10},{10,1... | collective-permute-start | bytes 786440 | tf_op jit(solution)/shard_map/ppermute | solution.py:342
  33.9 73.0 %collective-permute-start.3 = (bf16[16,8192]{1,0:T(8,128)(2,1)S(1)}, bf16[16,8192]{1,0:T(8,128)(2,1)S(1)}, u32[]{:S(2)}, u32[]{:S(2)}) collective-permute-start(bf16[16,8192]{1,0:T(8,128)(2,1)S(1)} %copy-done.2), channel_id=1, source_target_pairs={{1,0},{2,1},{3,2},{4,3},{5,4},{6,5},{7,6},{8,7},{9,8},{10,9},{11,1... | collective-permute-start | bytes 786440 | tf_op jit(solution)/shard_map/ppermute | solution.py:344
  107.0 0.7 copy-start.3
  107.0 0.8 copy-start.4
Sparse Core Ops, SparseCore 0:
  24.7 63.2 all-gather.2
where the time goes:
time: 133 us; the launch traced here: 130 us
  Pallas kernels  63.1 us (47%)
  waiting for transfers between devices  37.6 us (28%)
  starting transfers between devices  14.7 us (11%)
  between operations  13.5 us (10%)
  local copies, waits for them, and re-layouts  1.47 us (1%)
    pallas_call x4, Pallas kernels, call(): pl.pallas_call(body, out_shape=outs, in_specs=[smem] * scalars + [vmem] *...  63.1 us
    all_gather x1, waiting for transfers between devices, per_device(): roots = lax.all_gather(root, 'leaf')  37.5 us
    ppermute x1, starting transfers between devices, per_device(): pts_b = lax.ppermute(points, 'leaf', fall)  5.44 us
    ppermute x1, starting transfers between devices, per_device(): prb_b = lax.ppermute(probes, 'leaf', fall)  5.44 us
  transfers between devices with their start and end apart: 5, of which 1 were waited for; matrix products, arithmetic and copies ran while one was open for 1% of the time, Pallas kernels for 22%

commit v1 on v0

v1 whole, which is shorter than its diff:
```python
import math

import jax
import jax.numpy as jnp
from jax import lax
from jax.experimental import pallas as pl
from jax.experimental.pallas import tpu as pltpu
from jax.sharding import PartitionSpec as P

F32 = jnp.float32
BF16 = jnp.bfloat16
DEEP = 256
PIECE = 16
PAIRS = 2
VMEM_LIMIT = 56 * 1024 * 1024
MESH = pl.DeviceIdType.MESH


def mm(left, right):
    return jnp.dot(left, right, preferred_element_type=F32)


def mm_nt(left, right):
    return lax.dot_general(left, right, (((1,), (1,)), ((), ())), preferred_element_type=F32)


def split(value):
    high = value.astype(BF16)
    low = (value - high.astype(F32)).astype(BF16)
    return high, low


def affinity(scaled, emb_width):
    return jnp.exp2(scaled * (4.0 / emb_width * math.log2(math.e)))


def half_norms(pts):
    wide = pts.astype(F32)
    value = jnp.sum(wide * wide, axis=0, keepdims=True) * -0.5
    first = value.astype(BF16).astype(F32)
    rest = value - first
    second = rest.astype(BF16).astype(F32)
    third = (rest - second).astype(BF16).astype(F32)
    return first, second, third


def norm_rows(pieces, start):
    width = pieces[0].shape[1]
    row = lax.broadcasted_iota(jnp.int32, (PIECE, width), 0)
    rows = jnp.where(row < 6, 1.0, 0.0)
    for k, piece in enumerate(pieces):
        rows = jnp.where(row == start + k, piece, rows)
    return rows.astype(BF16)


def deep(*blocks):
    rows = sum(block.shape[0] for block in blocks)
    filler = jnp.zeros((DEEP - rows, blocks[0].shape[1]), BF16)
    return jnp.concatenate([*blocks, filler], axis=0)


def one_hot(pool, chosen):
    column = lax.broadcasted_iota(jnp.int32, (pool, chosen.shape[1]), 0)
    return jnp.where(column == chosen, 1.0, 0.0).astype(BF16)


def in_groups(total, size, step):
    size = min(size, total)
    if size == total:
        step(list(range(total)))
        return

    def body(i, carry):
        step([i * size + k for k in range(size)])
        return carry

    lax.fori_loop(0, total // size, body, 0)


def tree_node(first, second, first_q, second_q, chosen, emb_width):
    skel = first.shape[1]
    right_end = emb_width + PIECE
    joined = jnp.concatenate([first, second], axis=1)
    parent = mm(joined, one_hot(2 * skel, chosen)).astype(BF16)
    left = deep(joined[:emb_width], joined[right_end:]).T
    right = deep(jnp.concatenate([parent[:right_end], second[:right_end]], axis=1))
    raw = mm(left, right)
    up_high, up_low = split(affinity(raw[:, :skel], emb_width))
    joined_q = jnp.concatenate([first_q, second_q], axis=1)
    parent_q = (mm(joined_q, up_high) + mm(joined_q, up_low)).astype(BF16)
    cross_high, cross_low = split(affinity(raw[:skel, skel:], emb_width))
    couple_first = mm_nt(second_q, cross_high) + mm_nt(second_q, cross_low)
    couple_second = mm(first_q, cross_high) + mm(first_q, cross_low)
    return parent, parent_q, up_high, up_low, couple_first, couple_second


def spread_down(field, up_high, up_low):
    rows = field.shape[0]
    high, low = split(field)
    both = mm_nt(jnp.concatenate([high, low], axis=0), up_high)
    return both[:rows] + both[rows:] + mm_nt(high, up_low)


def tree_body(
    pts, prb, leaf_skel, local_skel, upper_skel,
    left, near, far, halo_pts, halo_prb,
    right_rows, lk_high, lk_low, up_high, up_low, couple, nodes, node_q,
    outbox, inbox, path_high, path_low, path_couple, fields,
    own_sem, halo_send, halo_recv, box_send, box_recv,
):
    emb_width = pts.shape[0]
    leaf_dev, skel = leaf_skel.shape
    leaf_len = pts.shape[1] // leaf_dev
    pts_rows = nodes.shape[1]
    levels = inbox.shape[0]
    dev_num = 1 << levels
    mine = lax.axis_index("leaf")
    bits = [lax.rem(lax.div(mine, 1 << level), 2) for level in range(levels)]
    partners = [mine + (1 - 2 * bits[level]) * (1 << level) for level in range(levels)]

    barrier = pltpu.get_barrier_semaphore()
    for peer in partners:
        pl.semaphore_signal(barrier, inc=1, device_id=(peer,), device_id_type=MESH)
    has_before = mine > 0
    has_after = mine < dev_num - 1
    crosses_before = jnp.logical_and(has_before, bits[0] == 0)
    crosses_after = jnp.logical_and(has_after, bits[0] == 1)

    @pl.when(crosses_before)
    def _():
        pl.semaphore_signal(barrier, inc=1, device_id=(mine - 1,), device_id_type=MESH)

    @pl.when(crosses_after)
    def _():
        pl.semaphore_signal(barrier, inc=1, device_id=(mine + 1,), device_id_type=MESH)

    pl.semaphore_wait(barrier, levels + jnp.where(jnp.logical_or(crosses_before, crosses_after), 1, 0))

    def halo_copy(which, source, target, slot, peer):
        return pltpu.make_async_remote_copy(
            src_ref=source, dst_ref=target.at[slot], send_sem=halo_send.at[which], recv_sem=halo_recv.at[which],
            device_id=(peer,), device_id_type=MESH,
        )

    to_after = [halo_copy(0, pts, halo_pts, 0, mine + 1), halo_copy(1, prb, halo_prb, 0, mine + 1)]
    to_before = [halo_copy(2, pts, halo_pts, 2, mine - 1), halo_copy(3, prb, halo_prb, 2, mine - 1)]

    @pl.when(has_after)
    def _():
        for copy in to_after:
            copy.start()

    @pl.when(has_before)
    def _():
        for copy in to_before:
            copy.start()

    own = [
        pltpu.make_async_copy(pts, halo_pts.at[1], own_sem.at[0]),
        pltpu.make_async_copy(prb, halo_prb.at[1], own_sem.at[1]),
    ]
    for copy in own:
        copy.start()

    def leaf_step(ids):
        done = []
        for i in ids:
            span = pl.ds(pl.multiple_of(i * leaf_len, leaf_len), leaf_len)
            tile = pts[:, span]
            pieces = half_norms(tile)
            right = norm_rows(pieces, 3)
            left_rows = norm_rows(pieces, 0)
            tile_left = deep(tile, left_rows).T
            stacked = jnp.concatenate([tile, right, left_rows], axis=0)
            node = mm(stacked, one_hot(leaf_len, leaf_skel[pl.ds(i, 1), :])).astype(BF16)
            raw = mm(tile_left, deep(node[: emb_width + PIECE]))
            high, low = split(affinity(raw, emb_width))
            tile_prb = prb[:, span]
            charge = (mm(tile_prb, high) + mm(tile_prb, low)).astype(BF16)
            done.append((span, right, tile_left, node, high, low, charge))
        for i, (span, right, tile_left, node, high, low, charge) in zip(ids, done):
            left[span, :] = tile_left
            right_rows[:, span] = right
            lk_high[span, :] = high
            lk_low[span, :] = low
            nodes[i] = node
            node_q[i] = charge

    in_groups(leaf_dev, 4, leaf_step)
    count = leaf_dev // 2
    row_base = 0
    while count:

        def level_step(ids, row_base=row_base):
            done = []
            for k in ids:
                row = row_base + k
                done.append(
                    tree_node(
                        nodes[2 * row], nodes[2 * row + 1], node_q[2 * row], node_q[2 * row + 1],
                        local_skel[pl.ds(row, 1), :], emb_width,
                    )
                )
            for k, (parent, parent_q, high, low, one, two) in zip(ids, done):
                row = row_base + k
                nodes[leaf_dev + row] = parent
                node_q[leaf_dev + row] = parent_q
                up_high[row] = high
                up_low[row] = low
                couple[2 * row] = one
                couple[2 * row + 1] = two

        in_groups(count, 4, level_step)
        row_base += count
        count //= 2
    top = 2 * leaf_dev - 2
    outbox[0, :pts_rows, :] = nodes[top]
    outbox[0, pts_rows:, :] = node_q[top]

    chunk = min(256, leaf_len)

    def own_pairs(i, carry):
        terms = []
        for k in range(PAIRS):
            leaf = i * PAIRS + k
            start = pl.multiple_of(leaf * leaf_len, leaf_len)
            span = pl.ds(start, leaf_len)
            right = deep(pts[:, span], right_rows[:, span])
            for at in range(0, leaf_len, chunk):
                part = left[pl.ds(pl.multiple_of(start + at, chunk), chunk), :]
                block = affinity(mm(part, right), emb_width).astype(BF16)
                terms.append((leaf, at, mm_nt(prb[:, span], block)))
        for leaf, at, term in terms:
            near[leaf, :, at : at + chunk] = term
        return carry

    groups = leaf_dev // PAIRS
    for level in range(levels):
        exchange = pltpu.make_async_remote_copy(
            src_ref=outbox.at[level], dst_ref=inbox.at[level],
            send_sem=box_send.at[level], recv_sem=box_recv.at[level],
            device_id=(partners[level],), device_id_type=MESH,
        )
        exchange.start()
        lax.fori_loop(level * groups // levels, (level + 1) * groups // levels, own_pairs, 0)
        exchange.wait()
        is_first = bits[level] == 0
        here = outbox[level]
        there = inbox[level]
        one = jnp.where(is_first, here, there)
        two = jnp.where(is_first, there, here)
        row = dev_num - (dev_num >> level) + lax.div(mine, 2 << level)
        parent, parent_q, high, low, couple_one, couple_two = tree_node(
            one[:pts_rows], two[:pts_rows], one[pts_rows:], two[pts_rows:],
            upper_skel[pl.ds(row, 1), :], emb_width,
        )
        path_high[level] = high
        path_low[level] = low
        path_couple[level] = jnp.where(is_first, couple_one, couple_two)
        if level < levels - 1:
            outbox[level + 1, :pts_rows, :] = parent
            outbox[level + 1, pts_rows:, :] = parent_q

    field = jnp.zeros(path_couple.shape[1:], F32)
    for level in reversed(range(levels)):
        spread = spread_down(field, path_high[level], path_low[level])
        field = jnp.where(bits[level] == 0, spread[:, :skel], spread[:, skel:]) + path_couple[level]
    fields[top] = field
    count = 1
    row_base = leaf_dev - 2
    while count < leaf_dev:

        def down_step(ids, row_base=row_base):
            done = []
            for k in ids:
                row = row_base + k
                spread = spread_down(fields[leaf_dev + row], up_high[row], up_low[row])
                done.append((spread[:, :skel] + couple[2 * row], spread[:, skel:] + couple[2 * row + 1]))
            for k, (one, two) in zip(ids, done):
                fields[2 * (row_base + k)] = one
                fields[2 * (row_base + k) + 1] = two

        in_groups(count, 4, down_step)
        count *= 2
        row_base -= count

    def far_step(ids):
        for i in ids:
            span = pl.ds(pl.multiple_of(i * leaf_len, leaf_len), leaf_len)
            far[:, span] = spread_down(fields[i], lk_high[span, :], lk_low[span, :])

    in_groups(leaf_dev, 4, far_step)
    for copy in own:
        copy.wait()

    @pl.when(has_after)
    def _():
        for copy in to_after:
            copy.wait_send()
        for copy in to_before:
            copy.wait_recv()

    @pl.when(has_before)
    def _():
        for copy in to_before:
            copy.wait_send()
        for copy in to_after:
            copy.wait_recv()


def list_pairs(near_list, near_count, base, targets, sources):
    leaf_dev = near_list.shape[0]

    def of_leaf(leaf, found):
        def of_slot(slot, found):
            targets[found] = leaf
            sources[found] = jnp.clip(near_list[leaf, slot] - base, 0, 3 * leaf_dev - 1)
            return found + 1

        return lax.fori_loop(1, near_count[leaf], of_slot, found)

    found = lax.fori_loop(0, leaf_dev, of_leaf, 0)
    for k in range(PAIRS - 1):
        targets[found + k] = leaf_dev
        sources[found + k] = leaf_dev
    return (found + PAIRS - 1) // PAIRS


def near_body(me, near_list, near_count, left, pts, prb, own, far, out, total, rows, targets, sources):
    leaf_dev = near_list.shape[0]
    leaf_len = total.shape[2]
    emb_width = pts.shape[1]
    chunk = min(256, leaf_len)
    total[:leaf_dev] = own[...]
    total[leaf_dev] = jnp.zeros(total.shape[1:], F32)
    steps = list_pairs(near_list, near_count, (me[0] - 1) * leaf_dev, targets, sources)

    def norms(ids):
        for i in ids:
            span = pl.ds(pl.multiple_of(i * leaf_len, leaf_len), leaf_len)
            for which in range(3):
                rows[which, :, span] = norm_rows(half_norms(pts[which, :, span]), 3)

    in_groups(leaf_dev, 2, norms)

    def step(i, carry):
        done = []
        for k in range(PAIRS):
            target = targets[i * PAIRS + k]
            source = sources[i * PAIRS + k]
            which = lax.div(source, leaf_dev)
            span = pl.ds(pl.multiple_of(lax.rem(source, leaf_dev) * leaf_len, leaf_len), leaf_len)
            right = deep(pts[which, :, span], rows[which, :, span])
            source_prb = prb[which, :, span]
            left_at = jnp.minimum(target, leaf_dev - 1) * leaf_len
            for at in range(0, leaf_len, chunk):
                part = left[pl.ds(pl.multiple_of(left_at + at, chunk), chunk), :]
                block = affinity(mm(part, right), emb_width).astype(BF16)
                done.append((target, at, mm_nt(source_prb, block)))
        for target, at, term in done:
            total[target, :, at : at + chunk] += term
        return carry

    lax.fori_loop(0, steps, step, 0)
    for leaf in range(leaf_dev):
        span = slice(leaf * leaf_len, (leaf + 1) * leaf_len)
        out[:, span] = total[leaf] + far[:, span]


def shape(dims, dtype):
    return jax.ShapeDtypeStruct(tuple(dims), dtype)


def per_device(points, probes, near_list, near_count, leaf_skel, local_skel, upper_skel):
    emb_width, shard_len = points.shape
    leaf_dev, slots = near_list.shape
    leaf_len = shard_len // leaf_dev
    skel = leaf_skel.shape[1]
    probe_num = probes.shape[0]
    levels = lax.axis_size("leaf").bit_length() - 1
    me = lax.axis_index("leaf").astype(jnp.int32).reshape(1)
    low_nodes = leaf_dev - 1
    all_nodes = 2 * leaf_dev - 1
    pts_rows = emb_width + 2 * PIECE
    vmem = pl.BlockSpec(memory_space=pltpu.VMEM)
    smem = pl.BlockSpec(memory_space=pltpu.SMEM)
    anywhere = pl.BlockSpec(memory_space=pl.ANY)
    left, near, far, halo_pts, halo_prb = pl.pallas_call(
        tree_body,
        out_shape=[
            shape((shard_len, DEEP), BF16),
            shape((leaf_dev, probe_num, leaf_len), F32),
            shape((probe_num, shard_len), F32),
            shape((3, emb_width, shard_len), BF16),
            shape((3, probe_num, shard_len), BF16),
        ],
        in_specs=[vmem] * 5,
        out_specs=[vmem] * 3 + [anywhere] * 2,
        scratch_shapes=[
            pltpu.VMEM((PIECE, shard_len), BF16),
            pltpu.VMEM((shard_len, skel), BF16),
            pltpu.VMEM((shard_len, skel), BF16),
            pltpu.VMEM((low_nodes, 2 * skel, skel), BF16),
            pltpu.VMEM((low_nodes, 2 * skel, skel), BF16),
            pltpu.VMEM((2 * low_nodes, probe_num, skel), F32),
            pltpu.VMEM((all_nodes, pts_rows, skel), BF16),
            pltpu.VMEM((all_nodes, probe_num, skel), BF16),
            pltpu.VMEM((levels, pts_rows + probe_num, skel), BF16),
            pltpu.VMEM((levels, pts_rows + probe_num, skel), BF16),
            pltpu.VMEM((levels, 2 * skel, skel), BF16),
            pltpu.VMEM((levels, 2 * skel, skel), BF16),
            pltpu.VMEM((levels, probe_num, skel), F32),
            pltpu.VMEM((all_nodes, probe_num, skel), F32),
            pltpu.SemaphoreType.DMA((2,)),
            pltpu.SemaphoreType.DMA((4,)),
            pltpu.SemaphoreType.DMA((4,)),
            pltpu.SemaphoreType.DMA((levels,)),
            pltpu.SemaphoreType.DMA((levels,)),
        ],
        compiler_params=pltpu.CompilerParams(
            vmem_limit_bytes=VMEM_LIMIT, collective_id=0, has_side_effects=True
        ),
        name="tree_and_halo",
    )(points, probes, leaf_skel, local_skel, upper_skel)

    pair_len = slots * leaf_dev + PAIRS
    return pl.pallas_call(
        near_body,
        out_shape=shape((probe_num, shard_len), F32),
        in_specs=[smem] * 3 + [vmem] * 5,
        out_specs=vmem,
        scratch_shapes=[
            pltpu.VMEM((leaf_dev + 1, probe_num, leaf_len), F32),
            pltpu.VMEM((3, PIECE, shard_len), BF16),
            pltpu.SMEM((pair_len,), jnp.int32),
            pltpu.SMEM((pair_len,), jnp.int32),
        ],
        compiler_params=pltpu.CompilerParams(vmem_limit_bytes=VMEM_LIMIT),
        name="near_field",
    )(me, near_list, near_count, left, halo_pts, halo_prb, near, far)


def solution(mesh):
    in_specs = (
        P(None, "leaf"),
        P(None, "leaf"),
        P("leaf", None),
        P("leaf"),
        P("leaf", None),
        P("leaf", None),
        P(),
    )
    return jax.shard_map(
        per_device, mesh=mesh, in_specs=in_specs, out_specs=P(None, "leaf"), check_vma=False
    )
```

time: 133 us -> 96.5 us (0.73); the launches traced: 130 us -> 96.5 us
  waiting for transfers between devices: 37.6 us -> 0 us
  Pallas kernels: 63.1 us -> 95.2 us
  starting transfers between devices: 14.7 us -> 0 us
  between operations: 13.5 us -> 0.01 us
    all_gather x1 -> x0, waiting for transfers between devices: 37.5 us -> none  [per_device(): roots = lax.all_gather(root, 'leaf')]
    pallas_call x4 -> x2, Pallas kernels: 63.1 us -> 95.2 us  [the longest x1 75.6 us: per_device(): pl.pallas_call(tree_body, out_shape=[shape((shard_len, DEEP), BF16), shap...]
    ppermute x4 -> x0, starting transfers between devices: 14.7 us -> none  [the longest x1 5.44 us: per_device(): pts_b = lax.ppermute(points, 'leaf', fall)]
  transfers between devices with their start and end apart: 5 -> 0, of which waited for: 1 -> 0; matrix products, arithmetic and copies ran while one was open for 1% -> 0% of each run, Pallas kernels for 22% -> 0%
where the time goes in v1:
time: 96.5 us
  Pallas kernels  95.2 us (99%)
  local copies, waits for them, and re-layouts  1.35 us (1%)
    pallas_call x1, Pallas kernels, per_device(): pl.pallas_call(tree_body, out_shape=[shape((shard_len, DEEP), BF16), shap...  75.6 us
    pallas_call x1, Pallas kernels, per_device(): pl.pallas_call(near_body, out_shape=shape((probe_num, shard_len), F32), i...  19.6 us

profile of v1, /device:TPU:16, one launch (start us, length us, event | category | flops | bytes accessed | tf_op | source)
XLA Modules:
  0.0 96.5 jit_solution(325995608468549474)
XLA Ops:
  0.0 1.4 %copy.8.near_list = s32[16,4]{1,0:T(8,128)} copy(s32[16,4]{0,1:T(4,128)} %param.9) | data formatting | bytes 512 | tf_op args[2]
  1.4 75.6 %tree_and_halo.1 = (bf16[8192,256]{1,0:T(8,128)(2,1)}, f32[16,16,512]{2,1,0:T(8,128)}, f32[16,8192]{1,0:T(8,128)}, bf16[3,128,8192]{2,1,0:T(8,128)(2,1)}, bf16[3,16,8192]{2,1,0:T(8,128)(2,1)}) custom-call(bf16[128,8192]{1,0:T(8,128)(2,1)} %pts.1, bf16[16,8192]{1,0:T(8,128)(2,1)} %prb.1, s32[16,128]{1,0:T(8,128)} %leaf_skel.1, s32[15,128]{1,0:T(8,128)} %local_skel.1, ...), custom_call_target="tpu_custom_call" | custom-call | tf_op jit(solution)/shard_map/tree_and_halo/pallas_call | solution.py:388
  76.9 19.6 %near_field.1 = f32[16,8192]{1,0:T(8,128)} custom-call(s32[1]{0:T(128)} %bitcast.me, s32[16,4]{1,0:T(8,128)} %copy.8.near_list, s32[16]{0:T(128)} %near_count.1, bf16[8192,256]{1,0:T(8,128)(2,1)} %get-tuple-element.10.left, bf16[3,128,8192]{2,1,0:T(8,128)(2,1)} %get-tuple-element.11.pts, bf16[3,16,8192]{2,1,0:T(8,128)(2,1)} %get-tuple-element.12.prb, ...), custom_call_target="tpu_custom_call" | custom-call | tf_op jit(solution)/shard_map/near_field/pallas_call | solution.py:427
